TPU v7x, 128 devices: a whole 4x4x4 slice. The times are simulated.
128 devices in a mesh: layer: 32 (over z, y, x_lo), row: 2 (over core), col: 2 (over x_hi).
Axes of the slice: x: 4 (x_hi: 2, x_lo: 2; x = x_hi * 2 + x_lo), y: 4, z: 4, core: 2. Of those that a mesh axis runs over, the one named last changes fastest.
Arguments:
- x_blocks: float32 [2, 64, 2, 6, 128, 128], P('row', 'layer', 'col'), may hold values from -0.3 to 0.3, as said below
- block_cols: int32 [2, 64, 2, 6], P('row', 'layer', 'col'), may hold values from 0 to 63, as said below
Outputs:
- x_next: float32 [2, 64, 2, 6, 128, 128], P('row', 'layer', 'col')
Inputs may be any that keep to these rules, and one draw needn't show every extreme that they name: `block_cols`: each tile q splits its 64 block indices into 32 groups of 2, numbered around a circle; a block row of tile r lying in group g has as its 6 columns in tile c exactly the members of groups g - 1, g and g + 1 (numbers taken around the circle) of tile c, in some order. So P is symmetric and holds every diagonal block. `x_blocks`: X is symmetric: the block stored at (n, k) is the transpose of the block stored at (k, n), and diagonal blocks are symmetric.
All inputs are finite; a program needn't handle non-finite values.
Results may differ from a plain program's by a relative error of at most 0.0003.
Values sent between devices are 32-bit elements; how exact they have to be, the bound alone decides.
A program may use at most 192 MiB of HBM per device.

v0:
```python
import jax
import jax.numpy as jnp
from jax import lax
from jax.sharding import PartitionSpec as P


def from_root(value, axis, source):
    kept = jnp.where(lax.axis_index(axis) == source, value, 0).astype(value.dtype)
    return lax.psum(kept, axis)


def pair_sum(left_blocks, left_ids, right_blocks, right_ids, pattern):
    highest = lax.Precision.HIGHEST
    tile_rows, slot_count = pattern.shape
    block_size = right_blocks.shape[-1]
    left_flat = left_blocks.reshape(-1, slot_count, block_size, block_size)
    right_flat = right_blocks.reshape(-1, slot_count, block_size, block_size)
    left_cols = left_ids.reshape(-1, slot_count)
    right_cols = right_ids.reshape(-1, slot_count)
    products = jnp.einsum("nsba,ntbc->nstac", left_flat, right_flat, precision=highest)
    row_pattern = jnp.take(pattern, left_cols, axis=0)
    matches = row_pattern[:, :, None, :] == right_cols[:, None, :, None]
    located = jnp.any(matches, axis=-1)
    position = jnp.sum(matches.astype(jnp.int32) * jnp.arange(slot_count, dtype=jnp.int32), axis=-1)
    outside = tile_rows * slot_count
    targets = jnp.where(located, left_cols[:, :, None] * slot_count + position, outside)
    summed = jax.ops.segment_sum(
        products.reshape(-1, block_size, block_size), targets.reshape(-1), num_segments=outside + 1
    )
    partial_value = summed[:outside].reshape(tile_rows, slot_count, block_size, block_size)
    return lax.psum_scatter(partial_value, "layer", scatter_dimension=0, tiled=True)


def body(x_blocks, block_cols):
    rows_dev = x_blocks.shape[1]
    slot_count = x_blocks.shape[3]
    block_size = x_blocks.shape[4]
    own_blocks = x_blocks.reshape(rows_dev, slot_count, block_size, block_size)
    own_ids = block_cols.reshape(rows_dev, slot_count)
    layer_here = lax.axis_index("layer")
    row_here = lax.axis_index("row")
    col_here = lax.axis_index("col")
    pattern = lax.all_gather(own_ids, "layer", axis=0, tiled=True)
    right_blocks, right_ids = (
        lax.all_gather(own_blocks[None], "row", axis=0, tiled=True),
        lax.all_gather(own_ids[None], "row", axis=0, tiled=True),
    )
    left_blocks, left_ids = (
        from_root(right_blocks, "col", row_here),
        from_root(right_ids, "col", row_here),
    )
    square = pair_sum(left_blocks, left_ids, right_blocks, right_ids, pattern)
    same_tile = row_here == col_here
    row_ids = layer_here * rows_dev + jnp.arange(rows_dev, dtype=jnp.int32)
    diagonal = ((own_ids == row_ids[:, None]) & same_tile).astype(jnp.float32)
    shifted = 3.0 * diagonal[:, :, None, None] * jnp.eye(block_size, dtype=jnp.float32) - square
    shifted_blocks = lax.all_gather(shifted[None], "row", axis=0, tiled=True)
    result = pair_sum(left_blocks, left_ids, shifted_blocks, right_ids, pattern)
    return (0.5 * result).reshape(1, rows_dev, 1, slot_count, block_size, block_size)


def solution(mesh):
    return jax.shard_map(
        body,
        mesh=mesh,
        in_specs=(P("row", "layer", "col", None, None, None), P("row", "layer", "col", None)),
        out_specs=P("row", "layer", "col", None, None, None),
        check_vma=False,
    )
```

profile of v0, /device:TPU:1, one launch (start us, length us, event | category | flops | bytes accessed | tf_op | source)
XLA Modules:
  0.0 1362.1 jit_solution(1507727140223230305)
XLA Ops:
  6.5 0.0 all-gather.7.cloned.1.call-start
  6.5 0.7 all-gather.7.cloned.1.call-update
  7.3 0.0 all-reduce.2.cloned.1.call-start
  7.3 17.9 %all-gather.7.cloned.1.call-done = f32[2,2,1,6,128,128]{5,4,3,2,1,0:T(8,128)} async-done(((f32[1,2,1,6,128,128]{5,4,3,2,1,0:T(8,128)}), f32[2,2,1,6,128,128]{5,4,3,2,1,0:T(8,128)}) %all-gather.7.cloned.1.call-update) | async-done | bytes 1572880 | tf_op jit(solution)/shard_map/all_gather | solution.py:45
  25.2 0.0 copy-start.1
  25.2 0.1 broadcast_select_fusion
  25.3 1.6 copy.29
  26.9 0.0 all-reduce.2.cloned.1.call-update
  27.0 0.0 reduce-scatter.3.cloned.1.call-start
  27.0 3.4 all-gather.1
  30.4 4.6 psum.14
  35.0 0.1 reshape.165
  35.1 67.8 %all-gather = s32[1,64,1,6]{3,2,0,1:T(1,128)S(1)} all-gather(s32[1,2,1,6]{3,2,0,1:T(1,128)} %bitcast.49), channel_id=2, replica_groups=mesh['layer'=32,'row'=2,'col'=2] {'layer'}, dimensions={1}, use_global_device_ids=true | all-gather | bytes 1584 | tf_op jit(solution)/shard_map/all_gather | solution.py:43
  102.9 0.6 gather_fusion
  103.5 0.1 copy.24
  103.5 0.1 reshape.168
  103.6 0.1 copy.25
  103.8 0.1 copy.26
  103.8 0.1 copy.27
  103.9 0.8 compare_reduce_fusion
  104.7 0.8 fusion.4
  105.5 0.1 copy.28
  105.6 0.1 reshape.140
  105.7 0.0 all-reduce.2.cloned.1.call-done
  105.7 0.0 copy-done.1
  105.8 11.0 fusion.2
  116.7 11.5 broadcast.72.clone
  128.3 29.6 %scatter_fusion = f32[385,128,128]{2,1,0:T(8,128)} fusion(f32[385,128,128]{2,1,0:T(8,128)} %broadcast.72.clone, s32[144]{0:T(256)S(1)} %reshape.140, f32[144,128,128]{2,1,0:T(8,128)} %bitcast.43), kind=kCustom, calls=%fused_computation.1 | custom fusion | flops 2359296 | bytes 28312128 | tf_op jit(solution)/shard_map/scatter-add | solution.py:27
  157.9 17.3 %slice.10 = f32[384,128,128]{2,1,0:T(8,128)} slice(f32[385,128,128]{2,1,0:T(8,128)} %scatter_fusion), slice={[0:384], [0:128], [0:128]} | slice | bytes 50331648 | tf_op jit(solution)/shard_map/slice | solution.py:30
  175.1 0.0 copy-start.2
  175.1 0.0 copy-start
  175.1 0.0 reduce-scatter.3.cloned.1.call-update
  175.2 0.0 all-gather.9.cloned.1.call-start
  175.2 0.6 copy-done.2
  175.8 0.1 and_select_fusion
  175.9 547.0 %reduce-scatter.3.cloned.1.call-done = f32[2,6,128,128]{3,2,1,0:T(8,128)} async-done(((f32[64,6,128,128]{3,2,1,0:T(8,128)}), f32[2,6,128,128]{3,2,1,0:T(8,128)}) %reduce-scatter.3.cloned.1.call-update) | async-done | bytes 786448 | tf_op jit(solution)/shard_map/reduce_scatter | solution.py:31
  722.8 2.1 multiply_subtract_fusion
  725.0 0.0 all-gather.9.cloned.1.call-update
  725.0 0.2 reduce-scatter.5.cloned.1.call-start
  725.2 11.3 all-gather.9.cloned.1.call-done
  736.6 0.0 copy-done
  736.6 11.1 convolution_bitcast_fusion
  747.6 9.6 copy.32
  757.2 11.5 broadcast.72
  768.8 29.6 %scatter_fusion.1 = f32[385,128,128]{2,1,0:T(8,128)} fusion(f32[385,128,128]{2,1,0:T(8,128)} %broadcast.72, s32[144]{0:T(256)S(1)} %reshape.140, f32[144,128,128]{2,1,0:T(8,128)} %bitcast.42), kind=kCustom, calls=%fused_computation.2 | custom fusion | flops 2359296 | bytes 28312128 | tf_op jit(solution)/shard_map/scatter-add | solution.py:27
  798.4 17.3 %slice.11 = f32[384,128,128]{2,1,0:T(8,128)} slice(f32[385,128,128]{2,1,0:T(8,128)} %scatter_fusion.1), slice={[0:384], [0:128], [0:128]} | slice | bytes 50331648 | tf_op jit(solution)/shard_map/slice | solution.py:30
  815.6 0.0 reduce-scatter.5.cloned.1.call-update
  815.6 537.9 %reduce-scatter.5.cloned.1.call-done = f32[2,6,128,128]{3,2,1,0:T(8,128)} async-done(((f32[64,6,128,128]{3,2,1,0:T(8,128)}), f32[2,6,128,128]{3,2,1,0:T(8,128)}) %reduce-scatter.5.cloned.1.call-update) | async-done | bytes 786448 | tf_op jit(solution)/shard_map/reduce_scatter | solution.py:31
  1353.5 2.1 multiply_bitcast_fusion
  (8 shorter events, 0.1 us)
Async XLA Ops:
  6.5 18.7 %all-gather.7.cloned.1.call-start = ((), (), s32[]{:S(2)}) async-start(), calls=%async_computation.5 | async-start | bytes 2359296 | tf_op jit(solution)/shard_map/all_gather | solution.py:45
  7.3 98.5 %all-reduce.2.cloned.1.call-start = ((), (), s32[]{:S(2)}) async-start(), calls=%async_computation.2 | async-start | bytes 3145728 | tf_op jit(solution)/shard_map/psum | solution.py:9
  25.2 80.6 %copy-start.1 = (f32[2,2,1,6,128,128]{5,4,3,2,1,0:T(8,128)S(1)}, f32[2,2,1,6,128,128]{5,4,3,2,1,0:T(8,128)}, u32[]{:S(2)}) copy-start(f32[2,2,1,6,128,128]{5,4,3,2,1,0:T(8,128)} %all-gather.7.cloned.1.call-done) | copy-start | bytes 4718596
  27.0 695.9 %reduce-scatter.3.cloned.1.call-start = ((), (), s32[]{:S(2)}) async-start(), calls=%async_computation.3 | async-start | bytes 25952256 | tf_op jit(solution)/shard_map/reduce_scatter | solution.py:31
  175.1 0.7 copy-start.2
  175.1 561.4 %copy-start = (f32[4,6,128,128]{2,3,1,0:T(8,128)S(1)}, f32[4,6,128,128]{2,3,1,0:T(8,128)}, u32[]{:S(2)}) copy-start(f32[4,6,128,128]{2,3,1,0:T(8,128)} %all-reduce.2.cloned.1.call-done) | copy-start | bytes 4718596
  175.2 561.4 %all-gather.9.cloned.1.call-start = ((), (), s32[]{:S(2)}) async-start(), calls=%async_computation.6 | async-start | bytes 2359296 | tf_op jit(solution)/shard_map/all_gather | solution.py:57
  725.0 628.5 %reduce-scatter.5.cloned.1.call-start = ((), (), s32[]{:S(2)}) async-start(), calls=%async_computation.4 | async-start | bytes 25952256 | tf_op jit(solution)/shard_map/reduce_scatter | solution.py:31
Sparse Core Ops, SparseCore 0:
  9.0 16.1 all-gather.6
  27.6 61.7 all-reduce.1
  175.3 547.5 reduce-scatter.2
  725.1 11.3 all-gather.8
  815.8 537.7 reduce-scatter.4
where the time goes:
time: 1360 us
  waiting for transfers between devices  1110 us (82%)
  blocking collectives  75.8 us (6%)
  local copies, waits for them, and re-layouts  70.7 us (5%)
  other arithmetic  65.1 us (5%)
  matrix products  22.1 us (2%)
    reduce_scatter x2, waiting for transfers between devices, pair_sum(): lax.psum_scatter(partial_value, 'layer', scatter_dimension=0, tiled=True)  1080 us
    all_gather x1, blocking collectives, body(): pattern = lax.all_gather(own_ids, 'layer', axis=0, tiled=True)  67.8 us
    scatter-add x2, other arithmetic, pair_sum(): jax.ops.segment_sum(products.reshape(-1, block_size, block_size), targets...  59.1 us
    slice x2, local copies, waits for them, and re-layouts, pair_sum(): summed[:outside].reshape(tile_rows, slot_count, block_size, block_size)  34.5 us
  transfers between devices with their start and end apart: 5, of which 4 were waited for; matrix products, arithmetic and copies ran while one was open for 0% of the time, Pallas kernels for 0%

commit v1 on v0

v1 whole, which is shorter than its diff:
```python
import functools

import jax
import jax.numpy as jnp
from jax import lax
from jax.experimental import pallas as pl
from jax.experimental.pallas import tpu as pltpu
from jax.sharding import PartitionSpec as P

MESH = pl.DeviceIdType.MESH
NL = 32
ROWS = 4
BLK = 128
VMEM_LIMIT = 56 * 1024 * 1024


def active_col(layer):
    return (layer // 8 + layer // 2) % 2


def my_ids():
    return lax.axis_index("layer"), lax.axis_index("row"), lax.axis_index("col")


def spread_kernel(x_ref, pat_ref, buf_ref, own_ref, other_ref, send, recv, psend, precv, local, core):
    me, row, col = my_ids()
    barrier = pltpu.get_barrier_semaphore()

    @pl.loop(1, NL)
    def _(k):
        p = lax.rem(me + k, NL)
        pl.semaphore_signal(barrier, inc=1, device_id=(p, row, col), device_id_type=MESH)

    pl.semaphore_signal(barrier, inc=1, device_id=(me, 1 - row, col), device_id_type=MESH)
    pl.semaphore_wait(barrier, NL)

    def pattern_copy(dst_owner, device, k):
        return pltpu.make_async_remote_copy(
            pat_ref, own_ref.at[dst_owner], psend.at[k], precv.at[dst_owner],
            device_id=(device, row, col), device_id_type=MESH)

    def data_copy(owner, device, k):
        return pltpu.make_async_remote_copy(
            x_ref.at[:, device], buf_ref.at[owner], send.at[k], recv.at[owner],
            device_id=(device, row, col), device_id_type=MESH)

    @pl.loop(1, NL)
    def _(k):
        pattern_copy(me, lax.rem(me + k, NL), k).start()

    @pl.loop(1, NL)
    def _(k):
        data_copy(me, lax.rem(me + k, NL), k).start()

    here = pltpu.make_async_copy(x_ref.at[:, me], buf_ref.at[me], local.at[0])
    here_pat = pltpu.make_async_copy(pat_ref, own_ref.at[me], local.at[1])
    here.start()
    here_pat.start()
    here_pat.wait()

    @pl.loop(1, NL)
    def _(k):
        p = lax.rem(me + k, NL)
        pattern_copy(p, p, k).wait_recv()

    swap = pltpu.make_async_remote_copy(
        own_ref, other_ref, core.at[0], core.at[1], device_id=(me, 1 - row, col), device_id_type=MESH)
    swap.start()

    @pl.loop(1, NL)
    def _(k):
        p = lax.rem(me + k, NL)
        data_copy(p, p, k).wait_recv()

    here.wait()
    swap.wait()

    @pl.loop(1, NL)
    def _(k):
        p = lax.rem(me + k, NL)
        pattern_copy(me, p, k).wait_send()
        data_copy(me, p, k).wait_send()


def dot_nt(a, b):
    return lax.dot_general(a, b, (((1,), (1,)), ((), ())), preferred_element_type=jnp.float32)


def dot_nn(a, b):
    return jnp.dot(a, b, preferred_element_type=jnp.float32)


def roll_groups(a, shift):
    return jnp.concatenate([a[shift:], a[:shift]], axis=0) if shift > 0 else jnp.concatenate([a[shift:], a[:shift]], axis=0)


def order_kernel(own_ref, other_ref, tin_ref, tout_ref):
    row = lax.axis_index("row")
    f32, bf16 = jnp.float32, jnp.bfloat16
    is_first = row == 0
    own = own_ref[...].astype(f32)
    other = other_ref[...].astype(f32)
    pat0 = jnp.where(is_first, own, other)
    pat1 = jnp.where(is_first, other, own)

    def rows_of(pat):
        return jnp.concatenate([pat[:, 0:6], pat[:, 6:12]], axis=0)

    def member(pat):
        iota = lax.broadcasted_iota(jnp.int32, (64, 64), 1).astype(f32)
        total = jnp.zeros((64, 64), f32)
        for s in range(6):
            total = total + jnp.where(pat[:, s:s + 1] == iota, 1.0, 0.0)
        return total

    def mask(cond):
        return jnp.where(cond, 1.0, 0.0)

    p0, p1 = rows_of(pat0), rows_of(pat1)
    m0, m1 = member(p0), member(p1)
    m0b, m1b = m0.astype(bf16), m1.astype(bf16)
    common = dot_nt(m0b, m0b)
    reach2 = mask(common > 1.0)
    b2 = reach2.astype(bf16)
    reach4 = mask(dot_nn(b2, b2) > 0.5)
    b4 = reach4.astype(bf16)
    b8 = mask(dot_nn(b4, b4) > 0.5).astype(bf16)
    lane = lax.broadcasted_iota(jnp.int32, (1, 64), 1).astype(f32)
    sub = lax.broadcasted_iota(jnp.int32, (64, 64), 0).astype(f32)
    first = common[0:1, :]
    start = jnp.min(jnp.where(first == 4.0, lane, 1000.0), axis=1, keepdims=True)
    second = jnp.sum(jnp.where(sub == start, common, 0.0), axis=0, keepdims=True)
    t = jnp.concatenate([mask(first > 5.0), mask(first > 3.0), mask(second > 5.0), mask(second > 3.0)], axis=0)
    for b in (b2, b4, b8):
        t = jnp.concatenate([t, mask(dot_nn(t.astype(bf16), b) > 0.5)], axis=0)
    which = lax.broadcasted_iota(jnp.int32, (32, 64), 0)
    from_first = jnp.bitwise_and(which, 3) < 2
    dist0 = 16.0 - jnp.sum(jnp.where(from_first, t, 0.0), axis=0, keepdims=True)
    dist1 = 16.0 - jnp.sum(jnp.where(from_first, 0.0, t), axis=0, keepdims=True)
    pos0 = jnp.where(dist1 < dist0, dist0, jnp.where(dist0 == 0.0, 0.0, 32.0 - dist0))
    group = lax.broadcasted_iota(jnp.int32, (32, 64), 0).astype(f32)
    g0 = mask(group == pos0)

    def centre(c):
        return mask(roll_groups(c, -1) + c + roll_groups(c, 1) > 5.0)

    hc = centre(dot_nn(g0.astype(bf16), m0b))
    g1 = centre(dot_nt(hc.astype(bf16), m1b))
    gr = jnp.where(is_first, g0, g1)
    pr = jnp.where(is_first, p0, p1)

    lanes = lax.broadcasted_iota(jnp.int32, (32, 64), 1)
    natural = (jnp.bitwise_and(lanes, 31) * 2 + jnp.right_shift(lanes, 5)).astype(f32)
    column = lanes.astype(f32)
    row_lo = jnp.min(jnp.where(gr > 0.5, natural, 1000.0), axis=1, keepdims=True)
    row_hi = jnp.max(jnp.where(gr > 0.5, natural, -1.0), axis=1, keepdims=True)
    col_lo = jnp.min(jnp.where(hc > 0.5, column, 1000.0), axis=1, keepdims=True)
    col_hi = jnp.max(jnp.where(hc > 0.5, column, -1.0), axis=1, keepdims=True)

    prb = jnp.concatenate([pr, jnp.zeros((64, 122), f32)], axis=1).astype(bf16)
    out_lane = lax.broadcasted_iota(jnp.int32, (32, 128), 1)
    slot_iota = out_lane.astype(f32)
    table = jnp.zeros((32, 128), f32)
    for a, members in enumerate((row_lo, row_hi)):
        chosen = mask((gr > 0.5) & (natural == members))
        cols = dot_nn(chosen.astype(bf16), prb)
        cols = jnp.where(out_lane < 6, cols, -1.0)
        for d in range(3):
            for j, cmem in enumerate((col_lo, col_hi)):
                target = roll_groups(cmem, d - 1) if d != 1 else cmem
                slot = jnp.sum(jnp.where(cols == target, slot_iota, 0.0), axis=1, keepdims=True)
                table = jnp.where(out_lane == a * 6 + d * 2 + j, members * 6.0 + slot, table)
    tin_ref[...] = table.astype(jnp.int32)

    eye = mask(lax.broadcasted_iota(jnp.int32, (64, 64), 0) == lax.broadcasted_iota(jnp.int32, (64, 64), 1)).astype(bf16)
    extra = lax.broadcasted_iota(jnp.int32, (32, 64), 0).astype(f32)
    grt = dot_nt(eye, gr.astype(bf16))
    gi = jnp.sum(grt * lax.broadcasted_iota(jnp.int32, (64, 32), 1).astype(f32), axis=1, keepdims=True)
    hi_flag = mask((gr > 0.5) & (natural == row_hi))
    ai = jnp.sum(dot_nt(eye, hi_flag.astype(bf16)), axis=1, keepdims=True)
    gcol = jnp.sum(hc * extra, axis=0, keepdims=True)
    jcol = jnp.sum(mask((hc > 0.5) & (column == col_hi)), axis=0, keepdims=True)
    code = gcol * 2.0 + jcol
    iota64 = lax.broadcasted_iota(jnp.int32, (64, 64), 1).astype(f32)
    lane64 = lax.broadcasted_iota(jnp.int32, (64, 128), 1)
    out = jnp.zeros((64, 128), jnp.int32)
    gi_i, ai_i = gi.astype(jnp.int32), ai.astype(jnp.int32)
    for s in range(6):
        val = jnp.sum(jnp.where(pr[:, s:s + 1] == iota64, code, 0.0), axis=1, keepdims=True).astype(jnp.int32)
        gc, jc = jnp.right_shift(val, 1), jnp.bitwise_and(val, 1)
        d = jnp.bitwise_and(gi_i - gc + 1, 31)
        out = jnp.where(lane64 == s, gc * 12 + d * 4 + ai_i * 2 + jc, out)
    tout_ref[...] = out


def deliver_kernel(tin_ref, buf_ref, x_ref, stage, send, recv, local, core):
    me, row, col = my_ids()
    active = active_col(me) == col
    barrier = pltpu.get_barrier_semaphore()

    @pl.when(active)
    def _():
        @pl.loop(1, NL)
        def _(k):
            p = lax.rem(me + k, NL)
            for c in range(2):
                pl.semaphore_signal(barrier, inc=1, device_id=(p, row, c), device_id_type=MESH)

        pl.semaphore_signal(barrier, inc=1, device_id=(me, row, 1 - col), device_id_type=MESH)
        pl.semaphore_signal(barrier, inc=1, device_id=(me, 1 - row, col), device_id_type=MESH)
        pl.semaphore_wait(barrier, NL)

    @pl.when(jnp.logical_not(active))
    def _():
        pl.semaphore_wait(barrier, NL)

    def fill(h):
        before, after = lax.rem(h + NL - 1, NL), lax.rem(h + 1, NL)
        for q in range(12):
            stage[h, q] = buf_ref[tin_ref[h, q]]
        for a in range(2):
            for j in range(2):
                stage[h, 12 + a * 2 + j] = buf_ref[tin_ref[before, a * 6 + 2 + j]]
                stage[h, 16 + a * 2 + j] = buf_ref[tin_ref[after, a * 6 + 2 + j]]

    def copy(h, source, source_col):
        return pltpu.make_async_remote_copy(
            stage.at[h], x_ref.at[row, source_col, :, source], send.at[h], recv.at[source_col, source],
            device_id=(h, row, active_col(h)), device_id_type=MESH)

    @pl.loop(1, NL)
    def _(k):
        h = lax.rem(me + k, NL)
        fill(h)
        copy(h, me, col).start()

    fill(me)
    here = pltpu.make_async_copy(stage.at[me], x_ref.at[row, col, :, me], local)

    @pl.when(active)
    def _():
        here.start()

    @pl.when(jnp.logical_not(active))
    def _():
        copy(me, me, col).start()

    @pl.when(active)
    def _():
        @pl.loop(1, NL)
        def _(k):
            p = lax.rem(me + k, NL)
            for c in range(2):
                copy(me, p, c).wait_recv()

        copy(me, me, 1 - col).wait_recv()
        here.wait()
        swap = pltpu.make_async_remote_copy(
            x_ref.at[row], x_ref.at[row], core.at[0], core.at[1],
            device_id=(me, 1 - row, col), device_id_type=MESH)
        swap.start()
        swap.wait()

    @pl.loop(1, NL)
    def _(k):
        h = lax.rem(me + k, NL)
        copy(h, me, col).wait_send()

    @pl.when(jnp.logical_not(active))
    def _():
        copy(me, me, col).wait_send()


def product_kernel(x_ref, y_ref, hi, lo, whi, wlo):
    row = lax.axis_index("row")
    bf16, f32 = jnp.bfloat16, jnp.float32

    def split(value):
        high = value.astype(bf16)
        return high, (value - high.astype(f32)).astype(bf16)

    for r in range(2):
        for c in range(2):
            for a in range(2):
                for j in range(2):
                    rows = pl.ds(r * 256 + a * 128, 128)
                    cols = pl.ds(c * 256 + j * 128, 128)
                    for part, q in enumerate((a * 6 + j, a * 6 + 2 + j, a * 6 + 4 + j, 12 + a * 2 + j, 16 + a * 2 + j)):
                        high, low = split(x_ref[r, c, q])
                        hi[part, rows, cols] = high
                        lo[part, rows, cols] = low

    def mul(pairs):
        total = None
        for (ah, al), part, transposed in pairs:
            dot = dot_nt if transposed else dot_nn
            bh, bl = hi[part], lo[part]
            term = dot(ah, bh) + dot(ah, bl) + dot(al, bh)
            total = term if total is None else total + term
        return total

    def apply(w):
        left, mid, right = w
        return (
            mul([(left, 3, False), (mid, 0, False)]),
            mul([(left, 0, True), (mid, 1, False), (right, 2, True)]),
            mul([(mid, 2, False), (right, 4, False)]),
        )

    mine = pl.ds(pl.multiple_of(row * 256, 256), 256)
    w = [(hi[part, mine, :], lo[part, mine, :]) for part in range(3)]
    left, mid, right = apply(w)
    q = lax.broadcasted_iota(jnp.int32, (256, 512), 0)
    k = lax.broadcasted_iota(jnp.int32, (256, 512), 1)
    mid = jnp.where(k == q + row * 256, 3.0, 0.0) - mid
    s = [split(-left), split(mid), split(-right)]
    y = apply(s)
    for d in range(3):
        half = 0.5 * y[d]
        for r in range(2):
            for a in range(2):
                for j in range(2):
                    block = half[j * 128:(j + 1) * 128, r * 256 + a * 128:r * 256 + (a + 1) * 128]
                    y_ref[r, d * 4 + a * 2 + j] = block.T


def home_kernel(tout_ref, y_ref, out_ref, sorted_ref, stage, send, recv, send2, recv2, local):
    me, row, col = my_ids()
    active = active_col(me) == col
    barrier = pltpu.get_barrier_semaphore()

    def source_of(h):
        return (h, col, active_col(h))

    self_source = jnp.logical_and(active, row == col)

    @pl.loop(1, NL)
    def _(k):
        p = lax.rem(me + k, NL)
        pl.semaphore_signal(barrier, inc=1, device_id=source_of(p), device_id_type=MESH)
        pl.semaphore_signal(barrier, inc=1, device_id=(p, row, col), device_id_type=MESH)

    @pl.when(jnp.logical_not(self_source))
    def _():
        pl.semaphore_signal(barrier, inc=1, device_id=source_of(me), device_id_type=MESH)

    @pl.when(jnp.logical_not(active))
    def _():
        pl.semaphore_wait(barrier, NL - 1)

    @pl.when(self_source)
    def _():
        pl.semaphore_wait(barrier, 3 * (NL - 1) + 1)

    @pl.when(jnp.logical_and(active, row != col))
    def _():
        pl.semaphore_wait(barrier, 3 * (NL - 1) + 2)

    def result_copy(p, r, source):
        return pltpu.make_async_remote_copy(
            y_ref.at[r, :, p], sorted_ref.at[source], send.at[r, p], recv.at[source],
            device_id=(p, r, row), device_id_type=MESH)

    here = pltpu.make_async_copy(y_ref.at[row, :, me], sorted_ref.at[me], local.at[0])

    @pl.when(active)
    def _():
        @pl.loop(1, NL)
        def _(k):
            p = lax.rem(me + k, NL)
            for r in range(2):
                result_copy(p, r, me).start()

        for r in range(2):
            @pl.when(jnp.logical_or(row != col, r != row))
            def _():
                result_copy(me, r, me).start()

        @pl.when(row == col)
        def _():
            here.start()

    @pl.loop(1, NL)
    def _(k):
        h = lax.rem(me + k, NL)
        result_copy(me, row, h).wait_recv()

    @pl.when(self_source)
    def _():
        here.wait()

    @pl.when(jnp.logical_not(self_source))
    def _():
        result_copy(me, row, me).wait_recv()

    def fill(l):
        for jj in range(2):
            for s in range(6):
                place = tout_ref[jj * 32 + l, s]
                stage[l, jj * 6 + s] = sorted_ref[place // 12, lax.rem(place, 12)]

    def home_copy(device, owner):
        return pltpu.make_async_remote_copy(
            stage.at[device], out_ref.at[:, owner], send2.at[device], recv2.at[owner],
            device_id=(device, row, col), device_id_type=MESH)

    @pl.loop(1, NL)
    def _(k):
        l = lax.rem(me + k, NL)
        fill(l)
        home_copy(l, me).start()

    fill(me)
    last = pltpu.make_async_copy(stage.at[me], out_ref.at[:, me], local.at[1])
    last.start()

    @pl.loop(1, NL)
    def _(k):
        p = lax.rem(me + k, NL)
        home_copy(p, p).wait_recv()

    last.wait()

    @pl.loop(1, NL)
    def _(k):
        p = lax.rem(me + k, NL)
        home_copy(p, me).wait_send()

    @pl.when(active)
    def _():
        @pl.loop(1, NL)
        def _(k):
            p = lax.rem(me + k, NL)
            for r in range(2):
                result_copy(p, r, me).wait_send()

        for r in range(2):
            @pl.when(jnp.logical_or(row != col, r != row))
            def _():
                result_copy(me, r, me).wait_send()


ANY = pl.BlockSpec(memory_space=pl.ANY)
VMEM = pl.BlockSpec(memory_space=pltpu.VMEM)
SMEM = pl.BlockSpec(memory_space=pltpu.SMEM)
DMA = pltpu.SemaphoreType.DMA


def params(collective_id):
    return pltpu.CompilerParams(collective_id=collective_id, has_side_effects=True, vmem_limit_bytes=VMEM_LIMIT)


def body(x_blocks, block_cols):
    f32 = jnp.float32
    x = x_blocks.reshape(12, NL, ROWS, BLK)
    pat = jnp.pad(block_cols.reshape(1, 12), ((0, 0), (0, 116)))
    buf, own, other = pl.pallas_call(
        spread_kernel,
        out_shape=(
            jax.ShapeDtypeStruct((NL, 12, ROWS, BLK), f32),
            jax.ShapeDtypeStruct((NL, 1, 128), jnp.int32),
            jax.ShapeDtypeStruct((NL, 1, 128), jnp.int32),
        ),
        in_specs=[ANY, ANY],
        out_specs=(ANY, ANY, ANY),
        scratch_shapes=[DMA((NL,)), DMA((NL,)), DMA((NL,)), DMA((NL,)), DMA((2,)), DMA((2,))],
        compiler_params=params(0),
        name="spread",
    )(x, pat)
    tin, tout = pl.pallas_call(
        order_kernel,
        out_shape=(jax.ShapeDtypeStruct((32, 128), jnp.int32), jax.ShapeDtypeStruct((64, 128), jnp.int32)),
        in_specs=[VMEM, VMEM],
        out_specs=(VMEM, VMEM),
        name="order",
    )(own.reshape(NL, 128), other.reshape(NL, 128))
    gathered = pl.pallas_call(
        deliver_kernel,
        out_shape=jax.ShapeDtypeStruct((2, 2, 20, NL, ROWS, BLK), f32),
        in_specs=[SMEM, VMEM],
        out_specs=ANY,
        scratch_shapes=[
            pltpu.VMEM((NL, 20, ROWS, BLK), f32), DMA((NL,)), DMA((2, NL)), DMA, DMA((2,))],
        compiler_params=params(1),
        name="deliver",
    )(tin, buf.reshape(NL * 12, ROWS, BLK))
    y = pl.pallas_call(
        product_kernel,
        out_shape=jax.ShapeDtypeStruct((2, 12, BLK, BLK), f32),
        in_specs=[VMEM],
        out_specs=VMEM,
        scratch_shapes=[
            pltpu.VMEM((5, 512, 512), jnp.bfloat16), pltpu.VMEM((5, 512, 512), jnp.bfloat16),
            pltpu.VMEM((256, 1536), jnp.bfloat16), pltpu.VMEM((256, 1536), jnp.bfloat16)],
        compiler_params=pltpu.CompilerParams(vmem_limit_bytes=VMEM_LIMIT),
        name="product",
    )(gathered.reshape(2, 2, 20, BLK, BLK))
    out = pl.pallas_call(
        home_kernel,
        out_shape=jax.ShapeDtypeStruct((12, NL, ROWS, BLK), f32),
        in_specs=[SMEM, ANY],
        out_specs=ANY,
        scratch_shapes=[
            pltpu.VMEM((NL, 12, ROWS, BLK), f32), pltpu.VMEM((NL, 12, ROWS, BLK), f32),
            DMA((2, NL)), DMA((NL,)), DMA((NL,)), DMA((NL,)), DMA((2,))],
        compiler_params=params(2),
        name="home",
    )(tout, y.reshape(2, 12, NL, ROWS, BLK))
    return out.reshape(x_blocks.shape)


def solution(mesh):
    return jax.shard_map(
        body,
        mesh=mesh,
        in_specs=(P("row", "layer", "col", None, None, None), P("row", "layer", "col", None)),
        out_specs=P("row", "layer", "col", None, None, None),
        check_vma=False,
    )
```

time: 1360 us -> 127 us (0.09)
  waiting for transfers between devices: 1110 us -> 0 us
  Pallas kernels: 0 us -> 122 us
  blocking collectives: 75.8 us -> 0 us
  local copies, waits for them, and re-layouts: 70.7 us -> 3.18 us
  other arithmetic: 65.1 us -> 1.34 us
  matrix products: 22.1 us -> 0 us
    reduce_scatter x2 -> x0, waiting for transfers between devices: 1080 us -> none  [pair_sum(): lax.psum_scatter(partial_value, 'layer', scatter_dimension=0, tiled=True)]
    pallas_call x0 -> x5, Pallas kernels: none -> 122 us  [the longest x1 45.7 us: body(): pl.pallas_call(deliver_kernel, out_shape=jax.ShapeDtypeStruct((2, 2, 20,...]
    all_gather x2 -> x0, blocking collectives: 71.2 us -> none  [the longest x1 67.8 us: body(): pattern = lax.all_gather(own_ids, 'layer', axis=0, tiled=True)]
    scatter-add x2 -> x0, other arithmetic: 59.1 us -> none  [pair_sum(): jax.ops.segment_sum(products.reshape(-1, block_size, block_size), targets...]
    slice x2 -> x0, local copies, waits for them, and re-layouts: 34.5 us -> none  [pair_sum(): summed[:outside].reshape(tile_rows, slot_count, block_size, block_size)]
    all_gather x2 -> x0, waiting for transfers between devices: 29.2 us -> none  [the longest x1 17.9 us: body(): lax.all_gather(own_blocks[None], 'row', axis=0, tiled=True)]
    another operation x2 -> x0, local copies, waits for them, and re-layouts: 23.1 us -> none
    dot_general x2 -> x0, matrix products: 22.1 us -> none  [pair_sum(): jnp.einsum('nsba,ntbc->nstac', left_flat, right_flat, precision=highest)]
  transfers between devices with their start and end apart: 5 -> 0, of which waited for: 4 -> 0; matrix products, arithmetic and copies ran while one was open for 0% -> 0% of each run, Pallas kernels for 0% -> 0%
where the time goes in v1:
time: 127 us; the launch traced here: 126 us
  Pallas kernels  122 us (96%)
  local copies, waits for them, and re-layouts  3.18 us (3%)
  other arithmetic  1.34 us (1%)
    pallas_call x1, Pallas kernels, body(): pl.pallas_call(deliver_kernel, out_shape=jax.ShapeDtypeStruct((2, 2, 20,...  45.7 us
    pallas_call x1, Pallas kernels, body(): pl.pallas_call(home_kernel, out_shape=jax.ShapeDtypeStruct((12, NL, ROWS,...  42.4 us
    pallas_call x1, Pallas kernels, body(): pl.pallas_call(spread_kernel, out_shape=(jax.ShapeDtypeStruct((NL, 12, RO...  20.7 us
    pallas_call x1, Pallas kernels, body(): pl.pallas_call(product_kernel, out_shape=jax.ShapeDtypeStruct((2, 12, BLK...  10.3 us
    pallas_call x1, Pallas kernels, body(): pl.pallas_call(order_kernel, out_shape=(jax.ShapeDtypeStruct((32, 128), j...  2.8 us
    unnamed x2, local copies, waits for them, and re-layouts  2.57 us

profile of v1, /device:TPU:1, one launch (start us, length us, event | category | flops | bytes accessed | tf_op | source)
XLA Modules:
  0.0 126.5 jit_solution(1554357319000120164)
XLA Ops:
  0.0 0.5 broadcast.5
  0.5 1.3 %reduce.3 = s32[2,6]{1,0:T(2,128)S(1)} reduce(s32[1,2,1,6]{3,2,1,0:T(1,128)} %param.3, s32[]{:T(128)} %broadcast.5), dimensions={0,2}, to_apply=%param.3.reduce_sub_computation.3 | reduce | bytes 100 | tf_op args[1]
  1.9 0.1 reshape.25
  1.9 0.5 pad.4.pat_ref
  2.5 20.7 %spread.1 = (f32[32,12,4,128]{3,2,1,0:T(4,128)}, s32[32,1,128]{2,1,0:T(1,128)}, s32[32,1,128]{2,1,0:T(1,128)}) custom-call(f32[12,32,4,128]{3,2,1,0:T(4,128)} %bitcast.12, s32[1,128]{1,0:T(1,128)} %pad.4.pat_ref), custom_call_target="tpu_custom_call" | custom-call | tf_op jit(solution)/shard_map/spread/pallas_call | solution.py:457
  23.1 2.8 %order.1 = (s32[32,128]{1,0:T(8,128)}, s32[64,128]{1,0:T(8,128)}) custom-call(s32[32,128]{1,0:T(8,128)} %bitcast.14, s32[32,128]{1,0:T(8,128)} %bitcast.15), custom_call_target="tpu_custom_call" | custom-call | tf_op jit(solution)/shard_map/order/pallas_call | solution.py:470
  25.9 45.7 %deliver.1 = f32[2,2,20,32,4,128]{5,4,3,2,1,0:T(4,128)} custom-call(s32[32,128]{1,0:T(8,128)} %get-tuple-element.13.tin_ref, f32[384,4,128]{2,1,0:T(4,128)} %bitcast.13), custom_call_target="tpu_custom_call" | custom-call | tf_op jit(solution)/shard_map/deliver/pallas_call | solution.py:477
  71.6 10.3 %product.1 = f32[2,12,128,128]{3,2,1,0:T(8,128)} custom-call(f32[2,2,20,128,128]{4,3,2,1,0:T(8,128)} %bitcast.9), custom_call_target="tpu_custom_call" | custom-call | tf_op jit(solution)/shard_map/product/pallas_call | solution.py:487
  81.9 42.4 %home.1 = f32[12,32,4,128]{3,2,1,0:T(4,128)} custom-call(s32[64,128]{1,0:T(8,128)} %get-tuple-element.12.tout_ref, f32[2,12,32,4,128]{4,3,2,1,0:T(4,128)} %bitcast.10), custom_call_target="tpu_custom_call" | custom-call | tf_op jit(solution)/shard_map/home/pallas_call | solution.py:498
  124.4 2.1 %copy.5 = f32[1,2,1,6,128,128]{5,4,3,2,1,0:T(8,128)} copy(f32[1,2,1,6,128,128]{5,4,3,2,1,0:T(8,128)} %bitcast.11) | data formatting | bytes 1572864

commit v2 on v0

v2 whole, which is shorter than its diff:
```python
import functools

import jax
import jax.numpy as jnp
from jax import lax
from jax.experimental import pallas as pl
from jax.experimental.pallas import tpu as pltpu
from jax.sharding import PartitionSpec as P

MESH = pl.DeviceIdType.MESH
NL = 32
ROWS = 4
BLK = 128
VMEM_LIMIT = 56 * 1024 * 1024


def my_ids():
    return lax.axis_index("layer"), lax.axis_index("row"), lax.axis_index("col")


def dot_nt(a, b):
    return lax.dot_general(a, b, (((1,), (1,)), ((), ())), preferred_element_type=jnp.float32)


def dot_nn(a, b):
    return jnp.dot(a, b, preferred_element_type=jnp.float32)


def roll_groups(a, shift):
    return jnp.concatenate([a[shift:], a[:shift]], axis=0)


def order_tables(row, own, other):
    f32, bf16 = jnp.float32, jnp.bfloat16
    is_first = row == 0
    own = own.astype(f32)
    other = other.astype(f32)
    pat0 = jnp.where(is_first, own, other)
    pat1 = jnp.where(is_first, other, own)

    def rows_of(pat):
        return jnp.concatenate([pat[:, 0:6], pat[:, 6:12]], axis=0)

    def member(pat):
        iota = lax.broadcasted_iota(jnp.int32, (64, 64), 1).astype(f32)
        total = jnp.zeros((64, 64), f32)
        for s in range(6):
            total = total + jnp.where(pat[:, s:s + 1] == iota, 1.0, 0.0)
        return total

    def mask(cond):
        return jnp.where(cond, 1.0, 0.0)

    p0, p1 = rows_of(pat0), rows_of(pat1)
    m0, m1 = member(p0), member(p1)
    m0b, m1b = m0.astype(bf16), m1.astype(bf16)
    common = dot_nt(m0b, m0b)
    reach2 = mask(common > 1.0)
    b2 = reach2.astype(bf16)
    reach4 = mask(dot_nn(b2, b2) > 0.5)
    b4 = reach4.astype(bf16)
    b8 = mask(dot_nn(b4, b4) > 0.5).astype(bf16)
    lane = lax.broadcasted_iota(jnp.int32, (1, 64), 1).astype(f32)
    sub = lax.broadcasted_iota(jnp.int32, (64, 64), 0).astype(f32)
    first = common[0:1, :]
    start = jnp.min(jnp.where(first == 4.0, lane, 1000.0), axis=1, keepdims=True)
    second = jnp.sum(jnp.where(sub == start, common, 0.0), axis=0, keepdims=True)
    t = jnp.concatenate([mask(first > 5.0), mask(first > 3.0), mask(second > 5.0), mask(second > 3.0)], axis=0)
    for b in (b2, b4, b8):
        t = jnp.concatenate([t, mask(dot_nn(t.astype(bf16), b) > 0.5)], axis=0)
    which = lax.broadcasted_iota(jnp.int32, (32, 64), 0)
    from_first = jnp.bitwise_and(which, 3) < 2
    dist0 = 16.0 - jnp.sum(jnp.where(from_first, t, 0.0), axis=0, keepdims=True)
    dist1 = 16.0 - jnp.sum(jnp.where(from_first, 0.0, t), axis=0, keepdims=True)
    pos0 = jnp.where(dist1 < dist0, dist0, jnp.where(dist0 == 0.0, 0.0, 32.0 - dist0))
    group = lax.broadcasted_iota(jnp.int32, (32, 64), 0).astype(f32)
    g0 = mask(group == pos0)

    def centre(c):
        return mask(roll_groups(c, -1) + c + roll_groups(c, 1) > 5.0)

    hc = centre(dot_nn(g0.astype(bf16), m0b))
    g1 = centre(dot_nt(hc.astype(bf16), m1b))
    gr = jnp.where(is_first, g0, g1)
    pr = jnp.where(is_first, p0, p1)

    lanes = lax.broadcasted_iota(jnp.int32, (32, 64), 1)
    natural = (jnp.bitwise_and(lanes, 31) * 2 + jnp.right_shift(lanes, 5)).astype(f32)
    column = lanes.astype(f32)
    row_lo = jnp.min(jnp.where(gr > 0.5, natural, 1000.0), axis=1, keepdims=True)
    row_hi = jnp.max(jnp.where(gr > 0.5, natural, -1.0), axis=1, keepdims=True)
    col_lo = jnp.min(jnp.where(hc > 0.5, column, 1000.0), axis=1, keepdims=True)
    col_hi = jnp.max(jnp.where(hc > 0.5, column, -1.0), axis=1, keepdims=True)

    prb = jnp.concatenate([pr, jnp.zeros((64, 122), f32)], axis=1).astype(bf16)
    out_lane = lax.broadcasted_iota(jnp.int32, (32, 128), 1)
    slot_iota = out_lane.astype(f32)
    table = jnp.zeros((32, 128), f32)
    for a, members in enumerate((row_lo, row_hi)):
        chosen = mask((gr > 0.5) & (natural == members))
        cols = dot_nn(chosen.astype(bf16), prb)
        cols = jnp.where(out_lane < 6, cols, -1.0)
        for d in range(3):
            for j, cmem in enumerate((col_lo, col_hi)):
                target = roll_groups(cmem, d - 1) if d != 1 else cmem
                slot = jnp.sum(jnp.where(cols == target, slot_iota, 0.0), axis=1, keepdims=True)
                table = jnp.where(out_lane == a * 6 + d * 2 + j, members * 6.0 + slot, table)
    tin = jnp.clip(table, 0.0, 383.0).astype(jnp.int32)

    eye = mask(lax.broadcasted_iota(jnp.int32, (64, 64), 0) == lax.broadcasted_iota(jnp.int32, (64, 64), 1)).astype(bf16)
    extra = lax.broadcasted_iota(jnp.int32, (32, 64), 0).astype(f32)
    grt = dot_nt(eye, gr.astype(bf16))
    gi = jnp.sum(grt * lax.broadcasted_iota(jnp.int32, (64, 32), 1).astype(f32), axis=1, keepdims=True)
    hi_flag = mask((gr > 0.5) & (natural == row_hi))
    ai = jnp.sum(dot_nt(eye, hi_flag.astype(bf16)), axis=1, keepdims=True)
    gcol = jnp.sum(hc * extra, axis=0, keepdims=True)
    jcol = jnp.sum(mask((hc > 0.5) & (column == col_hi)), axis=0, keepdims=True)
    code = gcol * 2.0 + jcol
    iota64 = lax.broadcasted_iota(jnp.int32, (64, 64), 1).astype(f32)
    lane64 = lax.broadcasted_iota(jnp.int32, (64, 128), 1)
    out = jnp.zeros((64, 128), jnp.int32)
    gi_i, ai_i = gi.astype(jnp.int32), ai.astype(jnp.int32)
    for s in range(6):
        val = jnp.sum(jnp.where(pr[:, s:s + 1] == iota64, code, 0.0), axis=1, keepdims=True).astype(jnp.int32)
        gc, jc = jnp.right_shift(val, 1), jnp.bitwise_and(val, 1)
        d = jnp.bitwise_and(gi_i - gc + 1, 31)
        out = jnp.where(lane64 == s, gc * 12 + jc * 6 + d * 2 + ai_i, out)
    return tin, jnp.clip(out, 0, 383)


def inside(place):
    return jnp.minimum(jnp.maximum(place, 0), NL * 12 - 1)


def split(value):
    high = value.astype(jnp.bfloat16)
    return high, (value - high.astype(jnp.float32)).astype(jnp.bfloat16)


def multiply(me, row, col, xs, hi, lo, y):
    @pl.loop(0, 16)
    def _(n):
        r, c, a, j = n // 8, lax.rem(n // 4, 2), lax.rem(n // 2, 2), lax.rem(n, 2)
        rows = pl.ds(pl.multiple_of(r * 256 + a * 128, 128), 128)
        cols = pl.ds(pl.multiple_of(c * 256 + j * 128, 128), 128)
        for part, q in enumerate((a * 6 + j, a * 6 + 2 + j, a * 6 + 4 + j, 12 + a * 2 + j, 16 + a * 2 + j)):
            high, low = split(xs[r, c, q].reshape(BLK, BLK))
            hi[part, rows, cols] = high
            lo[part, rows, cols] = low

    def mul(pairs):
        total = None
        for (stacked, high), part, transposed in pairs:
            dot = dot_nt if transposed else dot_nn
            both = dot(stacked, hi[part])
            term = both[:BLK] + both[BLK:] + dot(high, lo[part])
            total = term if total is None else total + term
        return total

    def apply(w):
        left, mid, right = w
        return (
            mul([(left, 3, False), (mid, 0, False)]),
            mul([(left, 0, True), (mid, 1, False), (right, 2, True)]),
            mul([(mid, 2, False), (right, 4, False)]),
        )

    def stack(high, low):
        return jnp.concatenate([high, low], axis=0), high

    offset = col * 256 + row * 128
    mine = pl.ds(pl.multiple_of(offset, 128), 128)
    left, mid, right = apply([stack(hi[part, mine, :], lo[part, mine, :]) for part in range(3)])
    q = lax.broadcasted_iota(jnp.int32, (BLK, 512), 0)
    k = lax.broadcasted_iota(jnp.int32, (BLK, 512), 1)
    mid = jnp.where(k == q + offset, 3.0, 0.0) - mid
    for d, part in enumerate(apply([stack(*split(-left)), stack(*split(mid)), stack(*split(-right))])):
        half = 0.5 * part
        for r in range(2):
            for a in range(2):
                first = r * 256 + a * 128
                y[r, d * 2 + a] = half[:, first:first + 128].T.reshape(NL, ROWS, BLK)


def kernel(
    cols_ref, x_ref, out_ref, pat, own, other, tin_v, tout_v, tin, tout, buf, stage, xs, hi, lo, y, srt, stage2,
    psend, precv, send1, recv1, send2, recv2, swap_send, swap_recv, send3, recv3, send4, recv4, core, local,
):
    me, row, col = my_ids()
    barrier = pltpu.get_barrier_semaphore()

    def signal(device):
        pl.semaphore_signal(barrier, inc=1, device_id=device, device_id_type=MESH)

    signal((me, 1 - row, col))
    signal((me, row, 1 - col))

    @pl.loop(1, NL)
    def _(k):
        signal((lax.rem(me + k, NL), row, col))

    for jj in range(2):
        pat[0:1, jj * 6:jj * 6 + 6] = cols_ref[0, jj]
    pl.semaphore_wait(barrier, NL + 1)

    def remote(src, dst, send, recv, device):
        return pltpu.make_async_remote_copy(src, dst, send, recv, device_id=device, device_id_type=MESH)

    def others(step):
        @pl.loop(1, NL)
        def _(k):
            step(lax.rem(me + k, NL))

    def pattern_copy(p, owner):
        return remote(pat, own.at[owner], psend.at[p], precv.at[owner], (p, row, col))

    def spread(p, owner):
        return remote(x_ref.at[:, p], buf.at[pl.ds(owner * 12, 12)], send1.at[p], recv1.at[owner], (p, row, col))

    others(lambda p: pattern_copy(p, me).start())
    others(lambda p: spread(p, me).start())
    here1 = pltpu.make_async_copy(x_ref.at[:, me], buf.at[pl.ds(me * 12, 12)], local.at[0])
    here1.start()
    own[me] = pat[...]
    others(lambda p: pattern_copy(p, p).wait_recv())
    swap_pattern = remote(own, other, core.at[0], core.at[1], (me, 1 - row, col))
    swap_pattern.start()
    swap_pattern.wait()
    tin_v[...], tout_v[...] = order_tables(row, own[...].reshape(NL, 128), other[...].reshape(NL, 128))
    for n, (vector, scalar) in enumerate(((tin_v, tin), (tout_v, tout))):
        move = pltpu.make_async_copy(vector, scalar, local.at[1 + n])
        move.start()
        move.wait()
    here1.wait()
    others(lambda p: spread(p, p).wait_recv())

    def deliver(h, c, source, source_col):
        return remote(
            stage.at[h], xs.at[row, source_col, :, source], send2.at[c, h], recv2.at[source_col, source], (h, row, c))

    def fill(h):
        before, after = lax.rem(h + NL - 1, NL), lax.rem(h + 1, NL)
        for q in range(12):
            stage[h, q] = buf[inside(tin[h, q])]
        for a in range(2):
            for j in range(2):
                stage[h, 12 + a * 2 + j] = buf[inside(tin[before, a * 6 + 2 + j])]
                stage[h, 16 + a * 2 + j] = buf[inside(tin[after, a * 6 + 2 + j])]

    @pl.loop(1, NL)
    def _(k):
        h = lax.rem(me + k, NL)
        fill(h)
        deliver(h, col, me, col).start()
        deliver(h, 1 - col, me, col).start()

    fill(me)
    deliver(me, 1 - col, me, col).start()
    here2 = pltpu.make_async_copy(stage.at[me], xs.at[row, col, :, me], local.at[3])
    here2.start()

    def swap(p, r):
        return remote(xs.at[r, :, :, p], xs.at[r, :, :, p], swap_send.at[p], swap_recv.at[p], (me, 1 - row, col))

    @pl.loop(1, NL)
    def _(k):
        p = lax.rem(me + NL - k, NL)
        deliver(me, col, p, 0).wait_recv()
        deliver(me, col, p, 1).wait_recv()
        swap(p, row).start()

    deliver(me, col, me, 1 - col).wait_recv()
    here2.wait()
    swap(me, row).start()

    @pl.loop(0, NL)
    def _(p):
        swap(p, 1 - row).wait_recv()

    multiply(me, row, col, xs, hi, lo, y)

    def result(p, r, source, member):
        return remote(y.at[r, :, p], srt.at[pl.ds(source * 12 + member * 6, 6)], send3.at[r, p], recv3.at[source, member], (p, r, col))

    @pl.loop(1, NL)
    def _(k):
        p = lax.rem(me + k, NL)
        result(p, row, me, row).start()
        result(p, 1 - row, me, row).start()

    result(me, 1 - row, me, row).start()
    here3 = pltpu.make_async_copy(y.at[row, :, me], srt.at[pl.ds(me * 12 + row * 6, 6)], local.at[4])
    here3.start()

    @pl.loop(1, NL)
    def _(k):
        h = lax.rem(me + NL - k, NL)
        result(me, row, h, 0).wait_recv()
        result(me, row, h, 1).wait_recv()

    result(me, row, me, 1 - row).wait_recv()
    here3.wait()

    def home(p, owner):
        return remote(stage2.at[p], out_ref.at[:, owner], send4.at[p], recv4.at[owner], (p, row, col))

    def fill_home(p):
        for jj in range(2):
            for s in range(6):
                stage2[p, jj * 6 + s] = srt[inside(tout[jj * 32 + p, s])]

    @pl.loop(1, NL)
    def _(k):
        p = lax.rem(me + k, NL)
        fill_home(p)
        home(p, me).start()

    fill_home(me)
    here4 = pltpu.make_async_copy(stage2.at[me], out_ref.at[:, me], local.at[5])
    here4.start()
    others(lambda p: home(p, p).wait_recv())
    here4.wait()

    @pl.loop(1, NL)
    def _(k):
        p = lax.rem(me + k, NL)
        pattern_copy(p, me).wait_send()
        spread(p, me).wait_send()
        deliver(p, col, me, col).wait_send()
        deliver(p, 1 - col, me, col).wait_send()
        swap(p, row).wait_send()
        result(p, 0, me, row).wait_send()
        result(p, 1, me, row).wait_send()
        home(p, me).wait_send()

    deliver(me, 1 - col, me, col).wait_send()
    swap(me, row).wait_send()
    result(me, 1 - row, me, row).wait_send()


ANY = pl.BlockSpec(memory_space=pl.ANY)
VMEM = pl.BlockSpec(memory_space=pltpu.VMEM)


def body(x_blocks, block_cols):
    f32, bf16, i32 = jnp.float32, jnp.bfloat16, jnp.int32
    vmem, smem, dma = pltpu.VMEM, pltpu.SMEM, pltpu.SemaphoreType.DMA
    out = pl.pallas_call(
        kernel,
        out_shape=jax.ShapeDtypeStruct((12, NL, ROWS, BLK), f32),
        in_specs=[VMEM, ANY],
        out_specs=ANY,
        scratch_shapes=[
            vmem((1, 128), i32), vmem((NL, 1, 128), i32), vmem((NL, 1, 128), i32),
            vmem((32, 128), i32), vmem((64, 128), i32), smem((32, 128), i32), smem((64, 128), i32),
            vmem((NL * 12, ROWS, BLK), f32), vmem((NL, 20, ROWS, BLK), f32), vmem((2, 2, 20, NL, ROWS, BLK), f32),
            vmem((5, 512, 512), bf16), vmem((5, 512, 512), bf16),
            vmem((2, 6, NL, ROWS, BLK), f32), vmem((NL * 12, ROWS, BLK), f32), vmem((NL, 12, ROWS, BLK), f32),
            dma((NL,)), dma((NL,)), dma((NL,)), dma((NL,)), dma((2, NL)), dma((2, NL)), dma((NL,)), dma((NL,)),
            dma((2, NL)), dma((NL, 2)), dma((NL,)), dma((NL,)), dma((2,)), dma((6,)),
        ],
        compiler_params=pltpu.CompilerParams(
            collective_id=0, has_side_effects=True, vmem_limit_bytes=VMEM_LIMIT),
        name="step",
    )(block_cols, x_blocks.reshape(12, NL, ROWS, BLK))
    return out.reshape(x_blocks.shape)


def solution(mesh):
    return jax.shard_map(
        body,
        mesh=mesh,
        in_specs=(P("row", "layer", "col", None, None, None), P("row", "layer", "col", None)),
        out_specs=P("row", "layer", "col", None, None, None),
        check_vma=False,
    )
```

time: 1360 us -> 102 us (0.07)
  waiting for transfers between devices: 1110 us -> 0 us
  Pallas kernels: 0 us -> 98.9 us
  blocking collectives: 75.8 us -> 0 us
  local copies, waits for them, and re-layouts: 70.7 us -> 2.06 us
  other arithmetic: 65.1 us -> 0 us
  matrix products: 22.1 us -> 0 us
    reduce_scatter x2 -> x0, waiting for transfers between devices: 1080 us -> none  [pair_sum(): lax.psum_scatter(partial_value, 'layer', scatter_dimension=0, tiled=True)]
    pallas_call x0 -> x1, Pallas kernels: none -> 98.9 us  [body(): pl.pallas_call(kernel, out_shape=jax.ShapeDtypeStruct((12, NL, ROWS, BLK)...]
    all_gather x2 -> x0, blocking collectives: 71.2 us -> none  [the longest x1 67.8 us: body(): pattern = lax.all_gather(own_ids, 'layer', axis=0, tiled=True)]
    scatter-add x2 -> x0, other arithmetic: 59.1 us -> none  [pair_sum(): jax.ops.segment_sum(products.reshape(-1, block_size, block_size), targets...]
    slice x2 -> x0, local copies, waits for them, and re-layouts: 34.5 us -> none  [pair_sum(): summed[:outside].reshape(tile_rows, slot_count, block_size, block_size)]
    all_gather x2 -> x0, waiting for transfers between devices: 29.2 us -> none  [the longest x1 17.9 us: body(): lax.all_gather(own_blocks[None], 'row', axis=0, tiled=True)]
    another operation x2 -> x0, local copies, waits for them, and re-layouts: 23.1 us -> none
    dot_general x2 -> x0, matrix products: 22.1 us -> none  [pair_sum(): jnp.einsum('nsba,ntbc->nstac', left_flat, right_flat, precision=highest)]
  transfers between devices with their start and end apart: 5 -> 0, of which waited for: 4 -> 0; matrix products, arithmetic and copies ran while one was open for 0% -> 0% of each run, Pallas kernels for 0% -> 0%
where the time goes in v2:
time: 102 us; the launch traced here: 101 us
  Pallas kernels  98.9 us (97%)
  local copies, waits for them, and re-layouts  2.06 us (2%)
    pallas_call x1, Pallas kernels, body(): pl.pallas_call(kernel, out_shape=jax.ShapeDtypeStruct((12, NL, ROWS, BLK)...  98.9 us
    unnamed x1, local copies, waits for them, and re-layouts  2.06 us

profile of v2, /device:TPU:1, one launch (start us, length us, event | category | flops | bytes accessed | tf_op | source)
XLA Modules:
  0.0 101.0 jit_solution(4501228523063230989)
XLA Ops:
  0.0 98.9 %step.1 = f32[12,32,4,128]{3,2,1,0:T(4,128)} custom-call(s32[1,2,1,6]{3,2,1,0:T(1,128)} %cols_ref.1, f32[12,32,4,128]{3,2,1,0:T(4,128)} %bitcast.5), custom_call_target="tpu_custom_call" | custom-call | tf_op jit(solution)/shard_map/step/pallas_call | solution.py:348
  99.0 2.1 %copy.5 = f32[1,2,1,6,128,128]{5,4,3,2,1,0:T(8,128)} copy(f32[1,2,1,6,128,128]{5,4,3,2,1,0:T(8,128)} %bitcast.4) | data formatting | bytes 1572864

commit v3 on v2

--- a/solution.py
+++ b/solution.py
@@ -11,6 +11,8 @@
 NL = 32
 ROWS = 4
 BLK = 128
+MAIN = 17
+SIDE = 14
 VMEM_LIMIT = 56 * 1024 * 1024
 
 
@@ -137,32 +139,58 @@
     return high, (value - high.astype(jnp.float32)).astype(jnp.bfloat16)
 
 
-def multiply(me, row, col, xs, hi, lo, y):
+def multiply(row, col, xs, hi, lo, y, send_half):
+    def put(part, r, a, c, j, block):
+        rows = pl.ds(pl.multiple_of(r * 256 + a * 128, 128), 128)
+        cols = pl.ds(pl.multiple_of(c * 256 + j * 128, 128), 128)
+        high, low = split(block)
+        hi[part, rows, cols] = high
+        lo[part, rows, cols] = low
+
+    def piece(r, n):
+        return xs[r, n].reshape(BLK, BLK)
+
     @pl.loop(0, 16)
     def _(n):
         r, c, a, j = n // 8, lax.rem(n // 4, 2), lax.rem(n // 2, 2), lax.rem(n, 2)
-        rows = pl.ds(pl.multiple_of(r * 256 + a * 128, 128), 128)
-        cols = pl.ds(pl.multiple_of(c * 256 + j * 128, 128), 128)
-        for part, q in enumerate((a * 6 + j, a * 6 + 2 + j, a * 6 + 4 + j, 12 + a * 2 + j, 16 + a * 2 + j)):
-            high, low = split(xs[r, c, q].reshape(BLK, BLK))
-            hi[part, rows, cols] = high
-            lo[part, rows, cols] = low
-
-    def mul(pairs):
+        base = MAIN * lax.rem(r + c, 2) + a * 2 + j
+        put(3, r, a, c, j, piece(r, base))
+        put(4, r, a, c, j, piece(r, base + 4))
+
+    @pl.loop(0, 3)
+    def _(part):
+        for r in range(2):
+            put(part, r, 0, r, 0, piece(r, 8 + part * 2))
+            mixed = piece(r, 9 + part * 2)
+            put(part, r, 0, r, 1, mixed)
+            put(part, r, 1, r, 0, mixed.T)
+            put(part, r, 1, r, 1, piece(r, 14 + part))
+            for e, (at, aj) in enumerate((((0, 0), (0, 1)), ((0, 1), (1, 1)))[r]):
+                block = piece(r, MAIN + 8 + part * 2 + e)
+                put(part, r, at, 1 - r, aj, block)
+                put(part, 1 - r, aj, r, at, block.T)
+
+    def mul(pairs, half=None):
         total = None
         for (stacked, high), part, transposed in pairs:
+            if half is None:
+                bh, bl = hi[part], lo[part]
+            elif transposed:
+                bh, bl = hi[part, half, :], lo[part, half, :]
+            else:
+                bh, bl = hi[part, :, half], lo[part, :, half]
             dot = dot_nt if transposed else dot_nn
-            both = dot(stacked, hi[part])
-            term = both[:BLK] + both[BLK:] + dot(high, lo[part])
+            both = dot(stacked, bh)
+            term = both[:BLK] + both[BLK:] + dot(high, bl)
             total = term if total is None else total + term
         return total
 
-    def apply(w):
+    def apply(w, half=None):
         left, mid, right = w
         return (
-            mul([(left, 3, False), (mid, 0, False)]),
-            mul([(left, 0, True), (mid, 1, False), (right, 2, True)]),
-            mul([(mid, 2, False), (right, 4, False)]),
+            mul([(left, 0, False), (mid, 3, False)], half),
+            mul([(left, 3, True), (mid, 1, False), (right, 4, True)], half),
+            mul([(mid, 4, False), (right, 2, False)], half),
         )
 
     def stack(high, low):
@@ -170,16 +198,17 @@
 
     offset = col * 256 + row * 128
     mine = pl.ds(pl.multiple_of(offset, 128), 128)
-    left, mid, right = apply([stack(hi[part, mine, :], lo[part, mine, :]) for part in range(3)])
+    left, mid, right = apply([stack(hi[part, mine, :], lo[part, mine, :]) for part in (3, 1, 4)])
     q = lax.broadcasted_iota(jnp.int32, (BLK, 512), 0)
     k = lax.broadcasted_iota(jnp.int32, (BLK, 512), 1)
     mid = jnp.where(k == q + offset, 3.0, 0.0) - mid
-    for d, part in enumerate(apply([stack(*split(-left)), stack(*split(mid)), stack(*split(-right))])):
-        half = 0.5 * part
-        for r in range(2):
+    s = [stack(*split(-left)), stack(*split(mid)), stack(*split(-right))]
+    for r in range(2):
+        for d, part in enumerate(apply(s, slice(r * 256, r * 256 + 256))):
+            half = 0.5 * part
             for a in range(2):
-                first = r * 256 + a * 128
-                y[r, d * 2 + a] = half[:, first:first + 128].T.reshape(NL, ROWS, BLK)
+                y[r, d * 2 + a] = half[:, a * 128:a * 128 + 128].T.reshape(NL, ROWS, BLK)
+        send_half(r)
 
 
 def kernel(
@@ -211,98 +240,123 @@
         def _(k):
             step(lax.rem(me + k, NL))
 
-    def pattern_copy(p, owner):
-        return remote(pat, own.at[owner], psend.at[p], precv.at[owner], (p, row, col))
-
-    def spread(p, owner):
-        return remote(x_ref.at[:, p], buf.at[pl.ds(owner * 12, 12)], send1.at[p], recv1.at[owner], (p, row, col))
-
-    others(lambda p: pattern_copy(p, me).start())
-    others(lambda p: spread(p, me).start())
+    def wait_bytes(ref, sem):
+        pltpu.make_async_copy(ref, ref, sem).wait()
+
+    def pattern_copy(p):
+        return remote(pat, own.at[me], psend, precv, (p, row, col))
+
+    def spread(p):
+        return remote(x_ref.at[:, p], buf.at[pl.ds(me * 12, 12)], send1, recv1, (p, row, col))
+
+    others(lambda p: pattern_copy(p).start())
+    others(lambda p: spread(p).start())
     here1 = pltpu.make_async_copy(x_ref.at[:, me], buf.at[pl.ds(me * 12, 12)], local.at[0])
     here1.start()
     own[me] = pat[...]
-    others(lambda p: pattern_copy(p, p).wait_recv())
+    wait_bytes(own.at[pl.ds(0, NL - 1)], precv)
     swap_pattern = remote(own, other, core.at[0], core.at[1], (me, 1 - row, col))
     swap_pattern.start()
     swap_pattern.wait()
     tin_v[...], tout_v[...] = order_tables(row, own[...].reshape(NL, 128), other[...].reshape(NL, 128))
-    for n, (vector, scalar) in enumerate(((tin_v, tin), (tout_v, tout))):
-        move = pltpu.make_async_copy(vector, scalar, local.at[1 + n])
+    moves = [
+        pltpu.make_async_copy(vector, scalar, local.at[1 + n])
+        for n, (vector, scalar) in enumerate(((tin_v, tin), (tout_v, tout)))
+    ]
+    for move in moves:
         move.start()
+    for move in moves:
         move.wait()
     here1.wait()
-    others(lambda p: spread(p, p).wait_recv())
-
-    def deliver(h, c, source, source_col):
+    wait_bytes(buf.at[pl.ds(0, (NL - 1) * 12)], recv1)
+
+    def deliver(h, c, source, same):
+        base, count = (0, MAIN) if same else (MAIN, SIDE)
         return remote(
-            stage.at[h], xs.at[row, source_col, :, source], send2.at[c, h], recv2.at[source_col, source], (h, row, c))
+            stage.at[h, pl.ds(0, count)], xs.at[row, pl.ds(base, count), source],
+            send2.at[c, h], recv2.at[1 - int(same), source], (h, row, c))
+
+    lower = row * (1 - col)
 
     def fill(h):
-        before, after = lax.rem(h + NL - 1, NL), lax.rem(h + 1, NL)
-        for q in range(12):
-            stage[h, q] = buf[inside(tin[h, q])]
         for a in range(2):
             for j in range(2):
-                stage[h, 12 + a * 2 + j] = buf[inside(tin[before, a * 6 + 2 + j])]
-                stage[h, 16 + a * 2 + j] = buf[inside(tin[after, a * 6 + 2 + j])]
-
-    @pl.loop(1, NL)
-    def _(k):
-        h = lax.rem(me + k, NL)
-        fill(h)
-        deliver(h, col, me, col).start()
-        deliver(h, 1 - col, me, col).start()
-
-    fill(me)
-    deliver(me, 1 - col, me, col).start()
-    here2 = pltpu.make_async_copy(stage.at[me], xs.at[row, col, :, me], local.at[3])
-    here2.start()
+                stage[h, a * 2 + j] = buf[inside(tin[h, a * 6 + j])]
+                stage[h, 4 + a * 2 + j] = buf[inside(tin[h, a * 6 + 4 + j])]
+        for n, g in enumerate((lax.rem(h + NL - 1, NL), h, lax.rem(h + 1, NL))):
+            stage[h, 8 + n * 2] = buf[inside(tin[g, 2 + lower])]
+            stage[h, 9 + n * 2] = buf[inside(tin[g, 3 + 6 * lower])]
+            stage[h, 14 + n] = buf[inside(tin[g, 9])]
+
+    def by_class(step):
+        for same in (True, False):
+            pl.when((row == col) if same else (row != col))(functools.partial(step, same))
+
+    def send_pieces(same):
+        @pl.loop(1, NL)
+        def _(k):
+            h = lax.rem(me + k, NL)
+            fill(h)
+            deliver(h, col, me, same).start()
+            deliver(h, 1 - col, me, same).start()
+
+        fill(me)
+        deliver(me, 1 - col, me, same).start()
+        base, count = (0, MAIN) if same else (MAIN, SIDE)
+        here = pltpu.make_async_copy(stage.at[me, pl.ds(0, count)], xs.at[row, pl.ds(base, count), me], local.at[3])
+        here.start()
+        here.wait()
+
+    by_class(send_pieces)
+    wait_bytes(own.at[pl.ds(0, NL - 1)], psend)
+    wait_bytes(buf.at[pl.ds(0, (NL - 1) * 12)], send1)
 
     def swap(p, r):
-        return remote(xs.at[r, :, :, p], xs.at[r, :, :, p], swap_send.at[p], swap_recv.at[p], (me, 1 - row, col))
+        return remote(xs.at[r, :, p], xs.at[r, :, p], swap_send, swap_recv, (me, 1 - row, col))
 
     @pl.loop(1, NL)
     def _(k):
         p = lax.rem(me + NL - k, NL)
-        deliver(me, col, p, 0).wait_recv()
-        deliver(me, col, p, 1).wait_recv()
+        deliver(me, col, p, True).wait_recv()
+        deliver(me, col, p, False).wait_recv()
         swap(p, row).start()
 
-    deliver(me, col, me, 1 - col).wait_recv()
-    here2.wait()
+    by_class(lambda same: deliver(me, col, me, not same).wait_recv())
     swap(me, row).start()
-
-    @pl.loop(0, NL)
-    def _(p):
-        swap(p, 1 - row).wait_recv()
-
-    multiply(me, row, col, xs, hi, lo, y)
-
-    def result(p, r, source, member):
-        return remote(y.at[r, :, p], srt.at[pl.ds(source * 12 + member * 6, 6)], send3.at[r, p], recv3.at[source, member], (p, r, col))
-
-    @pl.loop(1, NL)
-    def _(k):
-        p = lax.rem(me + k, NL)
-        result(p, row, me, row).start()
-        result(p, 1 - row, me, row).start()
-
-    result(me, 1 - row, me, row).start()
+    wait_bytes(xs.at[1 - row], swap_recv)
+
+    def result(p, r):
+        return remote(y.at[r, :, p], srt.at[pl.ds(me * 12 + row * 6, 6)], send3, recv3, (p, r, col))
+
     here3 = pltpu.make_async_copy(y.at[row, :, me], srt.at[pl.ds(me * 12 + row * 6, 6)], local.at[4])
-    here3.start()
-
-    @pl.loop(1, NL)
-    def _(k):
-        h = lax.rem(me + NL - k, NL)
-        result(me, row, h, 0).wait_recv()
-        result(me, row, h, 1).wait_recv()
-
-    result(me, row, me, 1 - row).wait_recv()
+
+    def send_half(r):
+        @pl.loop(1, NL)
+        def _(k):
+            result(lax.rem(me + k, NL), r).start()
+
+        @pl.when(r == row)
+        def _():
+            here3.start()
+
+        @pl.when(r != row)
+        def _():
+            result(me, r).start()
+
+    multiply(row, col, xs, hi, lo, y, send_half)
+
+    def sent_pieces(same):
+        others(lambda p: deliver(p, col, me, same).wait_send())
+        others(lambda p: deliver(p, 1 - col, me, same).wait_send())
+        deliver(me, 1 - col, me, same).wait_send()
+
+    by_class(sent_pieces)
+    wait_bytes(xs.at[row], swap_send)
     here3.wait()
-
-    def home(p, owner):
-        return remote(stage2.at[p], out_ref.at[:, owner], send4.at[p], recv4.at[owner], (p, row, col))
+    wait_bytes(srt.at[pl.ds(0, (2 * NL - 1) * 6)], recv3)
+
+    def home(p):
+        return remote(stage2.at[p], out_ref.at[:, me], send4, recv4, (p, row, col))
 
     def fill_home(p):
         for jj in range(2):
@@ -313,29 +367,15 @@
     def _(k):
         p = lax.rem(me + k, NL)
         fill_home(p)
-        home(p, me).start()
+        home(p).start()
 
     fill_home(me)
     here4 = pltpu.make_async_copy(stage2.at[me], out_ref.at[:, me], local.at[5])
     here4.start()
-    others(lambda p: home(p, p).wait_recv())
+    wait_bytes(srt.at[pl.ds(0, (2 * NL - 1) * 6)], send3)
+    wait_bytes(stage2.at[pl.ds(0, NL - 1)], send4)
     here4.wait()
-
-    @pl.loop(1, NL)
-    def _(k):
-        p = lax.rem(me + k, NL)
-        pattern_copy(p, me).wait_send()
-        spread(p, me).wait_send()
-        deliver(p, col, me, col).wait_send()
-        deliver(p, 1 - col, me, col).wait_send()
-        swap(p, row).wait_send()
-        result(p, 0, me, row).wait_send()
-        result(p, 1, me, row).wait_send()
-        home(p, me).wait_send()
-
-    deliver(me, 1 - col, me, col).wait_send()
-    swap(me, row).wait_send()
-    result(me, 1 - row, me, row).wait_send()
+    wait_bytes(stage2.at[pl.ds(0, NL - 1)], recv4)
 
 
 ANY = pl.BlockSpec(memory_space=pl.ANY)
@@ -353,11 +393,11 @@
         scratch_shapes=[
             vmem((1, 128), i32), vmem((NL, 1, 128), i32), vmem((NL, 1, 128), i32),
             vmem((32, 128), i32), vmem((64, 128), i32), smem((32, 128), i32), smem((64, 128), i32),
-            vmem((NL * 12, ROWS, BLK), f32), vmem((NL, 20, ROWS, BLK), f32), vmem((2, 2, 20, NL, ROWS, BLK), f32),
+            vmem((NL * 12, ROWS, BLK), f32), vmem((NL, MAIN, ROWS, BLK), f32), vmem((2, MAIN + SIDE, NL, ROWS, BLK), f32),
             vmem((5, 512, 512), bf16), vmem((5, 512, 512), bf16),
             vmem((2, 6, NL, ROWS, BLK), f32), vmem((NL * 12, ROWS, BLK), f32), vmem((NL, 12, ROWS, BLK), f32),
-            dma((NL,)), dma((NL,)), dma((NL,)), dma((NL,)), dma((2, NL)), dma((2, NL)), dma((NL,)), dma((NL,)),
-            dma((2, NL)), dma((NL, 2)), dma((NL,)), dma((NL,)), dma((2,)), dma((6,)),
+            dma, dma, dma, dma, dma((2, NL)), dma((2, NL)), dma, dma,
+            dma, dma, dma, dma, dma((2,)), dma((6,)),
         ],
         compiler_params=pltpu.CompilerParams(
             collective_id=0, has_side_effects=True, vmem_limit_bytes=VMEM_LIMIT),

time: 102 us -> 84.9 us (0.83)
  Pallas kernels: 98.9 us -> 82.7 us
    pallas_call x1, Pallas kernels: 98.9 us -> 82.7 us  [body(): pl.pallas_call(kernel, out_shape=jax.ShapeDtypeStruct((12, NL, ROWS, BLK)...]
where the time goes in v3:
time: 84.9 us; the launch traced here: 84.8 us
  Pallas kernels  82.7 us (97%)
  local copies, waits for them, and re-layouts  2.06 us (2%)
    pallas_call x1, Pallas kernels, body(): pl.pallas_call(kernel, out_shape=jax.ShapeDtypeStruct((12, NL, ROWS, BLK)...  82.7 us
    unnamed x1, local copies, waits for them, and re-layouts  2.06 us

profile of v3, /device:TPU:1, one launch (start us, length us, event | category | flops | bytes accessed | tf_op | source)
XLA Modules:
  0.0 84.8 jit_solution(10040387187917810685)
XLA Ops:
  0.0 82.7 %step.1 = f32[12,32,4,128]{3,2,1,0:T(4,128)} custom-call(s32[1,2,1,6]{3,2,1,0:T(1,128)} %cols_ref.1, f32[12,32,4,128]{3,2,1,0:T(4,128)} %bitcast.5), custom_call_target="tpu_custom_call" | custom-call | tf_op jit(solution)/shard_map/step/pallas_call | solution.py:388
  82.7 2.1 %copy.5 = f32[1,2,1,6,128,128]{5,4,3,2,1,0:T(8,128)} copy(f32[1,2,1,6,128,128]{5,4,3,2,1,0:T(8,128)} %bitcast.4) | data formatting | bytes 1572864

commit v4 on v3

--- a/solution.py
+++ b/solution.py
@@ -13,6 +13,7 @@
 BLK = 128
 MAIN = 17
 SIDE = 14
+STRIDE = 3
 VMEM_LIMIT = 56 * 1024 * 1024
 
 
@@ -240,6 +241,12 @@
         def _(k):
             step(lax.rem(me + k, NL))
 
+    def start_others(step):
+        @pl.loop(0, NL)
+        def _(k):
+            p = lax.rem(STRIDE * k + me, NL)
+            pl.when(p != me)(lambda: step(p))
+
     def wait_bytes(ref, sem):
         pltpu.make_async_copy(ref, ref, sem).wait()
 
@@ -249,8 +256,8 @@
     def spread(p):
         return remote(x_ref.at[:, p], buf.at[pl.ds(me * 12, 12)], send1, recv1, (p, row, col))
 
-    others(lambda p: pattern_copy(p).start())
-    others(lambda p: spread(p).start())
+    start_others(lambda p: pattern_copy(p).start())
+    start_others(lambda p: spread(p).start())
     here1 = pltpu.make_async_copy(x_ref.at[:, me], buf.at[pl.ds(me * 12, 12)], local.at[0])
     here1.start()
     own[me] = pat[...]
@@ -293,13 +300,12 @@
             pl.when((row == col) if same else (row != col))(functools.partial(step, same))
 
     def send_pieces(same):
-        @pl.loop(1, NL)
-        def _(k):
-            h = lax.rem(me + k, NL)
+        def step(h):
             fill(h)
             deliver(h, col, me, same).start()
             deliver(h, 1 - col, me, same).start()
 
+        start_others(step)
         fill(me)
         deliver(me, 1 - col, me, same).start()
         base, count = (0, MAIN) if same else (MAIN, SIDE)
@@ -331,9 +337,7 @@
     here3 = pltpu.make_async_copy(y.at[row, :, me], srt.at[pl.ds(me * 12 + row * 6, 6)], local.at[4])
 
     def send_half(r):
-        @pl.loop(1, NL)
-        def _(k):
-            result(lax.rem(me + k, NL), r).start()
+        start_others(lambda p: result(p, r).start())
 
         @pl.when(r == row)
         def _():
@@ -363,12 +367,11 @@
             for s in range(6):
                 stage2[p, jj * 6 + s] = srt[inside(tout[jj * 32 + p, s])]
 
-    @pl.loop(1, NL)
-    def _(k):
-        p = lax.rem(me + k, NL)
+    def go_home(p):
         fill_home(p)
         home(p).start()
 
+    start_others(go_home)
     fill_home(me)
     here4 = pltpu.make_async_copy(stage2.at[me], out_ref.at[:, me], local.at[5])
     here4.start()

time: 84.9 us -> 78.6 us (0.926)
  Pallas kernels: 82.7 us -> 76.4 us
    pallas_call x1, Pallas kernels: 82.7 us -> 76.4 us  [body(): pl.pallas_call(kernel, out_shape=jax.ShapeDtypeStruct((12, NL, ROWS, BLK)...]
where the time goes in v4:
time: 78.6 us; the launch traced here: 78.4 us
  Pallas kernels  76.4 us (97%)
  local copies, waits for them, and re-layouts  2.06 us (3%)
    pallas_call x1, Pallas kernels, body(): pl.pallas_call(kernel, out_shape=jax.ShapeDtypeStruct((12, NL, ROWS, BLK)...  76.4 us
    unnamed x1, local copies, waits for them, and re-layouts  2.06 us

profile of v4, /device:TPU:1, one launch (start us, length us, event | category | flops | bytes accessed | tf_op | source)
XLA Modules:
  0.0 78.4 jit_solution(18408066150877449708)
XLA Ops:
  0.0 76.4 %step.1 = f32[12,32,4,128]{3,2,1,0:T(4,128)} custom-call(s32[1,2,1,6]{3,2,1,0:T(1,128)} %cols_ref.1, f32[12,32,4,128]{3,2,1,0:T(4,128)} %bitcast.5), custom_call_target="tpu_custom_call" | custom-call | tf_op jit(solution)/shard_map/step/pallas_call | solution.py:391
  76.4 2.1 %copy.5 = f32[1,2,1,6,128,128]{5,4,3,2,1,0:T(8,128)} copy(f32[1,2,1,6,128,128]{5,4,3,2,1,0:T(8,128)} %bitcast.4) | data formatting | bytes 1572864

commit v5 on v4

--- a/solution.py
+++ b/solution.py
@@ -140,7 +140,7 @@
     return high, (value - high.astype(jnp.float32)).astype(jnp.bfloat16)
 
 
-def multiply(row, col, xs, hi, lo, y, send_half):
+def multiply(row, col, xs, hi, lo, y, wait_other, send_half):
     def put(part, r, a, c, j, block):
         rows = pl.ds(pl.multiple_of(r * 256 + a * 128, 128), 128)
         cols = pl.ds(pl.multiple_of(c * 256 + j * 128, 128), 128)
@@ -151,25 +151,29 @@
     def piece(r, n):
         return xs[r, n].reshape(BLK, BLK)
 
-    @pl.loop(0, 16)
-    def _(n):
-        r, c, a, j = n // 8, lax.rem(n // 4, 2), lax.rem(n // 2, 2), lax.rem(n, 2)
-        base = MAIN * lax.rem(r + c, 2) + a * 2 + j
-        put(3, r, a, c, j, piece(r, base))
-        put(4, r, a, c, j, piece(r, base + 4))
-
-    @pl.loop(0, 3)
-    def _(part):
-        for r in range(2):
+    def assemble(r):
+        @pl.loop(0, 8)
+        def _(n):
+            c, a, j = n // 4, lax.rem(n // 2, 2), lax.rem(n, 2)
+            base = MAIN * lax.rem(r + c, 2) + a * 2 + j
+            put(3, r, a, c, j, piece(r, base))
+            put(4, r, a, c, j, piece(r, base + 4))
+
+        @pl.loop(0, 3)
+        def _(part):
             put(part, r, 0, r, 0, piece(r, 8 + part * 2))
             mixed = piece(r, 9 + part * 2)
             put(part, r, 0, r, 1, mixed)
             put(part, r, 1, r, 0, mixed.T)
             put(part, r, 1, r, 1, piece(r, 14 + part))
-            for e, (at, aj) in enumerate((((0, 0), (0, 1)), ((0, 1), (1, 1)))[r]):
+            for e, (at, aj) in enumerate(((0, r), (r, 1))):
                 block = piece(r, MAIN + 8 + part * 2 + e)
                 put(part, r, at, 1 - r, aj, block)
                 put(part, 1 - r, aj, r, at, block.T)
+
+    assemble(row)
+    wait_other()
+    assemble(1 - row)
 
     def mul(pairs, half=None):
         total = None
@@ -244,7 +248,7 @@
     def start_others(step):
         @pl.loop(0, NL)
         def _(k):
-            p = lax.rem(STRIDE * k + me, NL)
+            p = lax.rem((STRIDE + 4 * row) * k + me, NL)
             pl.when(p != me)(lambda: step(p))
 
     def wait_bytes(ref, sem):
@@ -329,7 +333,6 @@
 
     by_class(lambda same: deliver(me, col, me, not same).wait_recv())
     swap(me, row).start()
-    wait_bytes(xs.at[1 - row], swap_recv)
 
     def result(p, r):
         return remote(y.at[r, :, p], srt.at[pl.ds(me * 12 + row * 6, 6)], send3, recv3, (p, r, col))
@@ -347,7 +350,7 @@
         def _():
             result(me, r).start()
 
-    multiply(row, col, xs, hi, lo, y, send_half)
+    multiply(row, col, xs, hi, lo, y, lambda: wait_bytes(xs.at[1 - row], swap_recv), send_half)
 
     def sent_pieces(same):
         others(lambda p: deliver(p, col, me, same).wait_send())

time: 78.6 us -> 77 us (0.980)
  Pallas kernels: 76.4 us -> 74.8 us
    pallas_call x1, Pallas kernels: 76.4 us -> 74.8 us  [body(): pl.pallas_call(kernel, out_shape=jax.ShapeDtypeStruct((12, NL, ROWS, BLK)...]
where the time goes in v5:
time: 77 us; the launch traced here: 76.9 us
  Pallas kernels  74.8 us (97%)
  local copies, waits for them, and re-layouts  2.06 us (3%)
    pallas_call x1, Pallas kernels, body(): pl.pallas_call(kernel, out_shape=jax.ShapeDtypeStruct((12, NL, ROWS, BLK)...  74.8 us
    unnamed x1, local copies, waits for them, and re-layouts  2.06 us

profile of v5, /device:TPU:1, one launch (start us, length us, event | category | flops | bytes accessed | tf_op | source)
XLA Modules:
  0.0 76.9 jit_solution(2457112206220682353)
XLA Ops:
  0.0 74.8 %step.1 = f32[12,32,4,128]{3,2,1,0:T(4,128)} custom-call(s32[1,2,1,6]{3,2,1,0:T(1,128)} %cols_ref.1, f32[12,32,4,128]{3,2,1,0:T(4,128)} %bitcast.5), custom_call_target="tpu_custom_call" | custom-call | tf_op jit(solution)/shard_map/step/pallas_call | solution.py:394
  74.8 2.1 %copy.5 = f32[1,2,1,6,128,128]{5,4,3,2,1,0:T(8,128)} copy(f32[1,2,1,6,128,128]{5,4,3,2,1,0:T(8,128)} %bitcast.4) | data formatting | bytes 1572864

commit v6 on v5

--- a/solution.py
+++ b/solution.py
@@ -306,8 +306,9 @@
     def send_pieces(same):
         def step(h):
             fill(h)
-            deliver(h, col, me, same).start()
-            deliver(h, 1 - col, me, same).start()
+            nearer = lax.rem(col + row, 2)
+            deliver(h, nearer, me, same).start()
+            deliver(h, 1 - nearer, me, same).start()
 
         start_others(step)
         fill(me)
@@ -386,6 +387,18 @@
 
 ANY = pl.BlockSpec(memory_space=pl.ANY)
 VMEM = pl.BlockSpec(memory_space=pltpu.VMEM)
+
+
+def finish(in_ref, out_ref, vm, sems, sems2):
+    first = [pltpu.make_async_copy(in_ref.at[pl.ds(2 * n, 2)], vm.at[pl.ds(2 * n, 2)], sems.at[n]) for n in range(6)]
+    second = [pltpu.make_async_copy(vm.at[pl.ds(2 * n, 2)], out_ref.at[pl.ds(2 * n, 2)], sems2.at[n]) for n in range(6)]
+    for part in first:
+        part.start()
+    for part, after in zip(first, second):
+        part.wait()
+        after.start()
+    for part in second:
+        part.wait()
 
 
 def body(x_blocks, block_cols):
@@ -409,6 +422,14 @@
             collective_id=0, has_side_effects=True, vmem_limit_bytes=VMEM_LIMIT),
         name="step",
     )(block_cols, x_blocks.reshape(12, NL, ROWS, BLK))
+    out = pl.pallas_call(
+        finish,
+        out_shape=jax.ShapeDtypeStruct((12, BLK, BLK), f32),
+        in_specs=[ANY],
+        out_specs=ANY,
+        scratch_shapes=[vmem((12, BLK, BLK), f32), dma((6,)), dma((6,))],
+        name="finish",
+    )(out.reshape(12, BLK, BLK))
     return out.reshape(x_blocks.shape)
 
 

time: 77 us -> 76.9 us (level)
  local copies, waits for them, and re-layouts: 2.06 us -> 0 us
  Pallas kernels: 74.8 us -> 76.8 us
    unnamed x1 -> x0, local copies, waits for them, and re-layouts: 2.06 us -> none
    pallas_call x0 -> x1, Pallas kernels: none -> 1.97 us  [body(): pl.pallas_call(finish, out_shape=jax.ShapeDtypeStruct((12, BLK, BLK), f32...]
where the time goes in v6:
time: 76.9 us; the launch traced here: 76.8 us
  Pallas kernels  76.8 us (100%)
    pallas_call x1, Pallas kernels, body(): pl.pallas_call(kernel, out_shape=jax.ShapeDtypeStruct((12, NL, ROWS, BLK)...  74.8 us
    pallas_call x1, Pallas kernels, body(): pl.pallas_call(finish, out_shape=jax.ShapeDtypeStruct((12, BLK, BLK), f32...  1.97 us

profile of v6, /device:TPU:1, one launch (start us, length us, event | category | flops | bytes accessed | tf_op | source)
XLA Modules:
  0.0 76.8 jit_solution(9953973204879766327)
XLA Ops:
  0.0 74.8 %step.1 = f32[12,32,4,128]{3,2,1,0:T(4,128)} custom-call(s32[1,2,1,6]{3,2,1,0:T(1,128)} %cols_ref.1, f32[12,32,4,128]{3,2,1,0:T(4,128)} %bitcast.6), custom_call_target="tpu_custom_call" | custom-call | tf_op jit(solution)/shard_map/step/pallas_call | solution.py:407
  74.8 2.0 %finish.1 = f32[12,128,128]{2,1,0:T(8,128)} custom-call(f32[12,128,128]{2,1,0:T(8,128)} %bitcast.5), custom_call_target="tpu_custom_call" | custom-call | tf_op jit(solution)/shard_map/finish/pallas_call | solution.py:425
